TPU v7x, 256 devices: a whole 4x4x8 slice. The times are simulated.
256 devices in a mesh: grp: 64 (over y, z, core), blk: 4 (over x).
Axes of the slice: x: 4, y: 4, z: 8, core: 2. Of those that a mesh axis runs over, the one named last changes fastest.
Arguments:
- visibility: bfloat16 [64, 4, 64, 32, 2048], P('grp', 'blk'), may hold values from -6 to 6
- block_group: int32 [4, 64], P('blk', 'grp'), may hold values from 0 to 1
- member_valid: int32 [4, 64, 32], P('blk', 'grp'), may hold values 0 or 1
Outputs:
- cross_power: float32 [4, 64, 4, 2, 32, 32, 128], P('blk', 'grp')
All inputs are finite; a program needn't handle non-finite values. No bound on the sum of `member_valid` on one device may be relied on, other than what follows from the above.
Results may differ from a plain program's by a relative error of at most 0.0039.
Values may be sent and summed in bfloat16 or wider, within the bound.
A program may use at most 128 MiB of HBM per device.

v0:
```python
import math

import jax
import jax.numpy as jnp
from jax import lax
from jax.sharding import PartitionSpec as P

DBAND = 128


def delay_table(channels, delay_band):
    channel_index = jnp.arange(channels, dtype=jnp.int32)
    delay_index = jnp.arange(delay_band, dtype=jnp.int32) - delay_band // 2
    angles = 2.0 * math.pi * channel_index.astype(jnp.float32) / channels
    window = (
        0.35875
        - 0.48829 * jnp.cos(angles)
        + 0.14128 * jnp.cos(2.0 * angles)
        - 0.01168 * jnp.cos(3.0 * angles)
    )
    turns = jnp.remainder(channel_index[:, None] * delay_index[None, :], channels).astype(
        jnp.float32
    )
    phases = 2.0 * math.pi * turns / channels
    scaling = window[:, None] / math.sqrt(channels)
    cosine = scaling * jnp.cos(phases)
    sine_part = scaling * jnp.sin(phases)
    upper_rows = jnp.concatenate([cosine, -sine_part], axis=1)
    lower_rows = jnp.concatenate([sine_part, cosine], axis=1)
    return jnp.concatenate([upper_rows, lower_rows], axis=0).astype(jnp.bfloat16)


def local(visibility, block_group, member_valid):
    table = delay_table(visibility.shape[-1] // 2, DBAND)
    local_spectra = jnp.dot(visibility, table, preferred_element_type=jnp.float32).astype(
        jnp.bfloat16
    )
    spectra = lax.all_to_all(local_spectra, "grp", split_axis=2, concat_axis=0, tiled=True)
    labels_sent = block_group.astype(jnp.bfloat16)
    flags_sent = member_valid.astype(jnp.bfloat16)
    partners, partner_labels, partner_flags = (
        lax.all_gather(spectra, "blk", axis=1, tiled=True),
        lax.all_gather(labels_sent, "blk", axis=0, tiled=True),
        lax.all_gather(flags_sent, "blk", axis=0, tiled=True),
    )
    own_spectra = spectra[:, 0, 0]
    other_spectra = partners[:, :, 0]
    own_real = own_spectra[..., :DBAND]
    own_imag = own_spectra[..., DBAND:]
    other_real = other_spectra[..., :DBAND]
    other_imag = other_spectra[..., DBAND:]
    cross_real = jnp.einsum(
        "tiq,tpjq->pijq", own_real, other_real, preferred_element_type=jnp.float32
    ) + jnp.einsum("tiq,tpjq->pijq", own_imag, other_imag, preferred_element_type=jnp.float32)
    cross_imag = jnp.einsum(
        "tiq,tpjq->pijq", own_imag, other_real, preferred_element_type=jnp.float32
    ) - jnp.einsum("tiq,tpjq->pijq", own_real, other_imag, preferred_element_type=jnp.float32)
    same_group = (partner_labels[:, 0] == labels_sent[0, 0]).astype(jnp.float32)
    own_valid = flags_sent[0, 0].astype(jnp.float32)
    other_valid = partner_flags[:, 0].astype(jnp.float32)
    keeping = same_group[:, None, None] * own_valid[None, :, None] * other_valid[:, None, :]
    total_times = spectra.shape[0]
    stacked = jnp.stack([cross_real, cross_imag], axis=1)
    result = stacked * keeping[:, None, :, :, None] / total_times
    return result[None, None]


def solution(mesh):
    in_specs = (P("grp", "blk", None, None, None), P("blk", "grp"), P("blk", "grp", None))
    out_specs = P("blk", "grp", None, None, None, None, None)
    return jax.shard_map(local, mesh=mesh, in_specs=in_specs, out_specs=out_specs, check_vma=False)
```

profile of v0, /device:TPU:1, one launch (start us, length us, event | category | flops | bytes accessed | tf_op | source)
XLA Modules:
  0.0 174.0 jit_solution(3091878308790678493)
XLA Ops:
  6.5 0.0 all-gather.3.cloned.1.call-start
  6.5 0.1 subtract_multiply_fusion
  6.6 2.3 %negate_convert_fusion = (bf16[1024,128]{1,0:T(8,128)(2,1)S(1)}, bf16[1024,128]{1,0:T(8,128)(2,1)S(1)}, bf16[1024,128]{1,0:T(8,128)(2,1)S(1)}) fusion(s32[128]{0:T(128)S(1)} %iota_add_fusion, f32[1024]{0:T(1024)S(1)} %subtract_multiply_fusion), kind=kLoop, calls=%fused_computation.25 | loop fusion | flops 2621440 | bytes 791040 | tf_op jit(solution)/shard_map/convert.8
  8.9 0.0 copy-start.7
  9.0 0.0 copy-start.6
  9.0 13.1 %fusion.6 = bf16[1,1,64,32,256]{4,2,3,1,0:T(8,128)(2,1)S(1)} fusion(bf16[64,32,2048]{2,1,0:T(8,128)(2,1)} %bitcast.72, bf16[1024,128]{1,0:T(8,128)(2,1)S(1)} %get-tuple-element.7, bf16[1024,128]{1,0:T(8,128)(2,1)S(1)} %get-tuple-element.6, bf16[1024,128]{1,0:T(8,128)(2,1)S(1)} %get-tuple-element.5), kind=kOutput, calls=%fused_computation.7 | convolution fusion | flops 2152202240 | bytes 10223616 | tf_op jit(solution)/shard_map/dot_general | solution.py:35
  22.0 0.6 copy.13
  22.6 41.7 %all_to_all.12 = bf16[1,1,64,32,256]{4,3,1,0,2:T(8,128)(2,1)S(1)} all-to-all(bf16[1,1,64,32,256]{4,3,1,0,2:T(8,128)(2,1)S(1)} %copy.13), channel_id=1, replica_groups=mesh['grp'=64,'blk'=4] {'grp'}, dimensions={2} | all-to-all | bytes 2097152 | tf_op jit(solution)/shard_map/all_to_all | solution.py:38
  64.3 1.6 copy.14
  65.9 0.0 all-gather.3.cloned.1.call-update
  66.6 0.0 copy-done.7
  66.6 0.6 dynamic-slice
  67.2 0.7 dynamic-update-slice
  68.0 8.5 %all-reduce = bf16[4]{0:T(256)(128)(2,1)S(1)} all-reduce(bf16[4]{0:T(256)(128)(2,1)S(1)} %dynamic-update-slice), channel_id=1, replica_groups=mesh['grp'=64,'blk'=4] {'blk'}, use_global_device_ids=true, to_apply=%add | all-reduce | flops 4 | bytes 16
  76.4 0.0 copy-done.6
  76.4 5.6 %all_gather.11 = bf16[4,1,32]{2,1,0:T(2,128)(2,1)S(1)} all-gather(bf16[1,1,32]{2,1,0:T(2,128)(2,1)S(1)} %get-tuple-element.9), channel_id=1, replica_groups=mesh['grp'=64,'blk'=4] {'blk'}, dimensions={0}, use_global_device_ids=true | all-gather | bytes 320 | tf_op jit(solution)/shard_map/all_gather | solution.py:44
  82.0 0.1 broadcast_multiply_fusion.1
  82.1 0.7 broadcast_multiply_fusion
  82.8 3.5 %copy.16 = bf16[1,1,64,32,256]{2,3,4,1,0:T(8,128)(2,1)S(1)} copy(bf16[1,1,64,32,256]{4,3,1,0,2:T(8,128)(2,1)S(1)} %all_to_all.12) | data formatting | bytes 2097152 | tf_op jit(solution)/shard_map/all_to_all | solution.py:38
  86.4 1.1 slice_bitcast_fusion.17
  87.4 1.1 slice_bitcast_fusion.14
  88.5 1.1 slice_bitcast_fusion.15
  89.6 1.0 slice_bitcast_fusion.16
  90.7 0.0 copy-start.4
  90.7 23.0 %all-gather.3.cloned.1.call-done = bf16[1,1,64,128,256]{4,2,1,0,3:T(8,128)(2,1)} async-done(((bf16[1,1,64,32,256]{4,2,1,0,3:T(8,128)(2,1)}), bf16[1,1,64,128,256]{4,2,1,0,3:T(8,128)(2,1)}) %all-gather.3.cloned.1.call-update) | async-done | bytes 4194320 | tf_op jit(solution)/shard_map/all_gather | solution.py:42
  113.7 13.0 %copy.15 = bf16[1,1,64,128,256]{2,3,4,1,0:T(8,128)(2,1)} copy(bf16[1,1,64,128,256]{4,2,1,0,3:T(8,128)(2,1)} %all-gather.3.cloned.1.call-done) | data formatting | bytes 8388608 | tf_op jit(solution)/shard_map/all_gather | solution.py:42
  126.7 0.0 copy-done.4
  126.7 0.0 copy-start.3
  126.7 3.5 %fusion.15 = f32[128,4,32,32]{3,2,1,0:T(8,128)S(1)} fusion(bf16[64,4,32,256]{0,2,1,3:T(8,128)(2,1)} %bitcast.63, bf16[64,32,128,1]{0,1,3,2:T(8,128)(2,1)S(1)} %copy-done.4), kind=kOutput, calls=%fused_computation.17 | convolution fusion | flops 67108864 | bytes 6815744 | tf_op jit(solution)/shard_map/tiq,tpjq->pijq/dot_general | solution.py:52
  130.2 0.0 copy-done.3
  130.2 6.7 %add_bitcast_fusion = f32[1,1,4,1,32,32,128]{4,5,2,6,3,1,0:T(8,128)} fusion(f32[128,4,32,32]{3,2,1,0:T(8,128)S(1)} %fusion.15, bf16[64,4,32,256]{0,2,1,3:T(8,128)(2,1)} %bitcast.64, bf16[64,32,128,1]{0,1,3,2:T(8,128)(2,1)S(1)} %copy-done.3), kind=kOutput, calls=%fused_computation.3 | convolution fusion | flops 67633152 | bytes 8912896 | tf_op jit(solution)/shard_map/tiq,tpjq->pijq/dot_general | solution.py:54
  136.9 0.0 copy-start.2
  136.9 8.1 %copy.17 = f32[1,1,4,1,32,32,128]{6,5,4,3,2,1,0:T(8,128)} copy(f32[1,1,4,1,32,32,128]{4,5,2,6,3,1,0:T(8,128)} %add_bitcast_fusion) | data formatting | bytes 4194304 | tf_op jit(solution)/shard_map/stack | solution.py:63
  145.0 0.0 copy-done.2
  145.0 0.0 copy-start.1
  145.0 3.5 %fusion.16 = f32[128,4,32,32]{3,2,1,0:T(8,128)S(1)} fusion(bf16[64,4,32,256]{0,2,1,3:T(8,128)(2,1)} %bitcast.65, bf16[64,32,128,1]{0,1,3,2:T(8,128)(2,1)S(1)} %copy-done.2), kind=kOutput, calls=%fused_computation.18 | convolution fusion | flops 67108864 | bytes 6815744 | tf_op jit(solution)/shard_map/tiq,tpjq->pijq/dot_general | solution.py:55
  148.5 0.0 copy-done.1
  148.5 6.7 %subtract_bitcast_fusion = f32[1,1,4,1,32,32,128]{4,5,2,6,3,1,0:T(8,128)} fusion(f32[128,4,32,32]{3,2,1,0:T(8,128)S(1)} %fusion.16, bf16[64,4,32,256]{0,2,1,3:T(8,128)(2,1)} %bitcast.66, bf16[64,32,128,1]{0,1,3,2:T(8,128)(2,1)S(1)} %copy-done.1), kind=kOutput, calls=%fused_computation.2 | convolution fusion | flops 67633152 | bytes 8912896 | tf_op jit(solution)/shard_map/tiq,tpjq->pijq/dot_general | solution.py:57
  155.3 0.0 copy-start
  155.3 0.0 copy-start.5
  155.3 8.2 %copy.18 = f32[1,1,4,1,32,32,128]{6,5,4,3,2,1,0:T(8,128)} copy(f32[1,1,4,1,32,32,128]{4,5,2,6,3,1,0:T(8,128)} %subtract_bitcast_fusion) | data formatting | bytes 4194304 | tf_op jit(solution)/shard_map/stack | solution.py:63
  163.4 0.0 copy-done
  163.4 0.0 copy-done.5
  163.4 3.7 %fusion.2 = f32[1,1,4,2,32,32,128]{6,5,4,3,2,1,0:T(8,128)} fusion(f32[1,1,4,1,32,32,128]{6,5,4,3,2,1,0:T(8,128)} %copy.18, f32[1,1,4,1,32,32,128]{6,5,4,3,2,1,0:T(8,128)S(1)} %copy-done, f32[4,32,32]{2,1,0:T(8,128)S(1)} %copy-done.5), kind=kLoop, calls=%fused_computation.5 | loop fusion | flops 3145728 | bytes 8404992 | tf_op jit(solution)/shard_map/div | solution.py:64
  (5 shorter events, 0.0 us)
Async XLA Ops:
  6.5 107.2 %all-gather.3.cloned.1.call-start = ((), (), s32[]{:S(2)}) async-start(), calls=%async_computation.1 | async-start | bytes 5242880 | tf_op jit(solution)/shard_map/all_gather | solution.py:42
  8.9 57.6 %copy-start.7 = (u32[256]{0:T(256)S(1)}, u32[256]{0:T(256)}, u32[]{:S(2)}) copy-start(u32[256]{0:T(256)} %constant.52) | copy-start | bytes 3076
  9.0 67.5 %copy-start.6 = (s32[1,1,32]{2,1,0:T(1,128)S(1)}, s32[1,1,32]{2,1,0:T(1,128)}, u32[]{:S(2)}) copy-start(s32[1,1,32]{2,1,0:T(1,128)} %param.5) | copy-start | bytes 388
  90.7 36.0 %copy-start.4 = (bf16[64,32,128,1]{0,1,3,2:T(8,128)(2,1)S(1)}, bf16[64,32,128,1]{0,1,3,2:T(8,128)(2,1)}, u32[]{:S(2)}) copy-start(bf16[64,32,128,1]{0,1,3,2:T(8,128)(2,1)} %slice_bitcast_fusion.16) | copy-start | bytes 1572868
  126.7 3.5 %copy-start.3 = (bf16[64,32,128,1]{0,1,3,2:T(8,128)(2,1)S(1)}, bf16[64,32,128,1]{0,1,3,2:T(8,128)(2,1)}, u32[]{:S(2)}) copy-start(bf16[64,32,128,1]{0,1,3,2:T(8,128)(2,1)} %slice_bitcast_fusion.15) | copy-start | bytes 1572868
  136.9 8.1 %copy-start.2 = (bf16[64,32,128,1]{0,1,3,2:T(8,128)(2,1)S(1)}, bf16[64,32,128,1]{0,1,3,2:T(8,128)(2,1)}, u32[]{:S(2)}) copy-start(bf16[64,32,128,1]{0,1,3,2:T(8,128)(2,1)} %slice_bitcast_fusion.17) | copy-start | bytes 1572868
  145.0 3.5 %copy-start.1 = (bf16[64,32,128,1]{0,1,3,2:T(8,128)(2,1)S(1)}, bf16[64,32,128,1]{0,1,3,2:T(8,128)(2,1)}, u32[]{:S(2)}) copy-start(bf16[64,32,128,1]{0,1,3,2:T(8,128)(2,1)} %slice_bitcast_fusion.14) | copy-start | bytes 1572868
  155.3 8.2 %copy-start = (f32[1,1,4,1,32,32,128]{6,5,4,3,2,1,0:T(8,128)S(1)}, f32[1,1,4,1,32,32,128]{6,5,4,3,2,1,0:T(8,128)}, u32[]{:S(2)}) copy-start(f32[1,1,4,1,32,32,128]{6,5,4,3,2,1,0:T(8,128)} %copy.17) | copy-start | bytes 6291460
  155.3 8.2 %copy-start.5 = (f32[4,32,32]{2,1,0:T(8,128)S(1)}, f32[4,32,32]{2,1,0:T(8,128)}, u32[]{:S(2)}) copy-start(f32[4,32,32]{2,1,0:T(8,128)} %broadcast_multiply_fusion) | copy-start | bytes 49156
Sparse Core Ops, SparseCore 0:
  66.0 47.6 all-gather.2
where the time goes:
time: 175 us; the launch traced here: 174 us
  blocking collectives  55.7 us (32%)
  local copies, waits for them, and re-layouts  40.6 us (23%)
  matrix products  33.5 us (19%)
  waiting for transfers between devices  23.1 us (13%)
  between operations  14.1 us (8%)
  other arithmetic  6.88 us (4%)
    all_to_all x1, blocking collectives, local(): lax.all_to_all(local_spectra, 'grp', split_axis=2, concat_axis=0, tiled=T...  41.7 us
    all_gather x1, waiting for transfers between devices, local(): lax.all_gather(spectra, 'blk', axis=1, tiled=True)  23 us
    another operation x2, local copies, waits for them, and re-layouts, local(): stacked = jnp.stack([cross_real, cross_imag], axis=1)  16.3 us
    dot_general x1, matrix products, local(): jnp.dot(visibility, table, preferred_element_type=jnp.float32)  13.1 us
    all_gather x1, local copies, waits for them, and re-layouts, local(): lax.all_gather(spectra, 'blk', axis=1, tiled=True)  13 us
    unnamed x1, blocking collectives  8.46 us
    dot_general x1, matrix products, local(): jnp.einsum('tiq,tpjq->pijq', own_imag, other_imag, preferred_element_type...  6.72 us
    dot_general x1, matrix products, local(): jnp.einsum('tiq,tpjq->pijq', own_real, other_imag, preferred_element_type...  6.72 us
  transfers between devices with their start and end apart: 1, of which 1 were waited for; matrix products, arithmetic and copies ran while one was open for 6% of the time, Pallas kernels for 0%

commit v1 on v0

v1 whole, which is shorter than its diff:
```python
import functools
import math

import jax
import jax.numpy as jnp
import numpy as np
import ml_dtypes
from jax import lax
from jax.experimental import pallas as pl
from jax.experimental.pallas import tpu as pltpu
from jax.sharding import PartitionSpec as P

MESH = pl.DeviceIdType.MESH
F32 = jnp.float32
BF16 = jnp.bfloat16

CH = 1024
DBAND = 128
MB = 32
NT = 64
NB = 4
NY, NZ = 4, 8
ROWS = 64
LANES = 128
NR = DBAND // 4
CHUNK = 8
NCHUNK = NT // CHUNK
NPAIR = NT // 2
LAG = 8


def delay_table():
    f = np.arange(CH)
    angles = 2.0 * math.pi * f / CH
    window = (
        0.35875
        - 0.48829 * np.cos(angles)
        + 0.14128 * np.cos(2.0 * angles)
        - 0.01168 * np.cos(3.0 * angles)
    ).astype(np.float32)
    d = np.arange(DBAND) - DBAND // 2
    phases = 2.0 * math.pi * ((f[:, None] * d[None, :]) % CH) / CH
    scaling = window[:, None].astype(np.float64) / math.sqrt(CH)
    c, s = scaling * np.cos(phases), scaling * np.sin(phases)
    real = np.concatenate([c, s], axis=0)
    imag = np.concatenate([-s, c], axis=0)
    both = np.stack([real, imag], axis=2).reshape(2 * CH, NR, 4, 2)
    rows = both.transpose(2, 1, 3, 0).reshape(2 * DBAND, 2 * CH)
    return rows.astype(np.float32).astype(ml_dtypes.bfloat16)


def group_masks(shape):
    group = lax.broadcasted_iota(jnp.int32, shape, 1) // MB
    return [group == h for h in range(4)]


def pick(masks, values):
    out = values[3]
    for h in (2, 1, 0):
        out = jnp.where(masks[h], values[h], out)
    return out


def exchange_kernel(
    vis, table, valid, label, gathered, flags,
    vis_v, table_v, valid_v, label_v, turned, send, own_flags,
    vis_sem, table_sem, valid_sem, label_sem, own_sem, flag_own_sem,
    a_s, a_r, x_s, x_r, f_s, f_r, g_s, g_r,
):
    g = lax.axis_index("grp")
    x = lax.axis_index("blk")
    y, z, zh, zl = g // 16, (g // 2) % 8, (g // 8) % 2, (g // 2) % 4
    right, left = (x + 1) % 4, (x + 3) % 4

    def chunk_of(k):
        return ((y + k // 2) % 4) * 2 + (zh + k) % 2

    def vis_copy(k):
        rows = pl.ds(pl.multiple_of(chunk_of(k) * CHUNK * MB, CHUNK * MB), CHUNK * MB)
        return pltpu.make_async_copy(vis.at[rows], vis_v.at[k], vis_sem.at[k])

    table_copy = pltpu.make_async_copy(table, table_v, table_sem)
    valid_copy = pltpu.make_async_copy(valid, valid_v, valid_sem)
    label_copy = pltpu.make_async_copy(label, label_v, label_sem)
    table_copy.start()
    valid_copy.start()
    label_copy.start()
    for k in range(NCHUNK):
        vis_copy(k).start()

    barrier = pltpu.get_barrier_semaphore()

    def greet(i, _):
        pl.semaphore_signal(barrier, inc=1, device_id=((g + i) % NT, x), device_id_type=MESH)
        return 0

    lax.fori_loop(1, NT, greet, 0)
    for o in range(1, NB):
        pl.semaphore_signal(barrier, inc=1, device_id=(g, (x + o) % NB), device_id_type=MESH)

    valid_copy.wait()
    label_copy.wait()
    own_flags[...] = jnp.zeros_like(own_flags)
    own_flags[0:1, :] = jnp.concatenate([valid_v[...]] * 4, axis=1)
    own_flags[1:2, :] = jnp.broadcast_to(label_v[...], (1, LANES))
    table_copy.wait()

    def send_copy(t):
        return pltpu.make_async_remote_copy(
            src_ref=send.at[t], dst_ref=gathered.at[0, g],
            send_sem=a_s.at[t], recv_sem=a_r.at[g],
            device_id=(t, x), device_id_type=MESH,
        )

    def arrival(t):
        return pltpu.make_async_remote_copy(
            src_ref=send.at[t], dst_ref=gathered.at[0, t],
            send_sem=a_s.at[t], recv_sem=a_r.at[t],
            device_id=(t, x), device_id_type=MESH,
        )

    own_copy = pltpu.make_async_copy(send.at[g], gathered.at[0, g], own_sem)
    flag_own = pltpu.make_async_copy(own_flags, flags.at[0], flag_own_sem)
    masks = group_masks((ROWS, LANES))

    def flag_copy(o):
        return pltpu.make_async_remote_copy(
            src_ref=own_flags, dst_ref=flags.at[o],
            send_sem=g_s.at[o], recv_sem=g_r.at[o],
            device_id=(g, (x + NB - o) % NB), device_id_type=MESH,
        )

    def transform(k, _):
        vis_copy(k).wait()
        chunk = chunk_of(k)
        turned[...] = lax.dot_general(
            table_v[...], vis_v[k], (((1,), (1,)), ((), ())), preferred_element_type=F32
        )
        for half in range(2):
            lanes = slice(half * LANES, (half + 1) * LANES)
            parts = [
                turned[pl.ds(pl.multiple_of(((h + NB - x) % 4) * ROWS, ROWS), ROWS), lanes]
                for h in range(4)
            ]
            rolled = []
            for d in range(4):
                v = pick(masks, [parts[(c + d) % 4] for c in range(4)])
                rolled.append(pltpu.roll(v, MB * d, 1) if d else v)
            for c in range(4):
                block = pick(masks, [rolled[(h - c) % 4] for h in range(4)])
                send[chunk * CHUNK + half * 4 + c] = block.astype(BF16)

        @pl.when(k == 0)
        def _():
            pl.semaphore_wait(barrier, NT - 1 + NB - 1)
            own_copy.start()
            flag_own.start()
            for o in range(1, NB):
                flag_copy(o).start()

        for dz in range(4):
            for core in range(2):
                t = chunk * CHUNK + ((zl + dz) % 4) * 2 + core

                @pl.when(t != g)
                def _():
                    send_copy(t).start()

        return 0

    lax.fori_loop(0, NCHUNK, transform, 0)

    def pair_of(k):
        step, dz = k // 4, k % 4
        return ((y + 4 - step // 2) % 4) * 16 + ((zh + step) % 2) * 8 + ((zl + 4 - dz) % 4) * 2

    def x_copy(k, d):
        times = pl.ds(pair_of(k), 2)
        return pltpu.make_async_remote_copy(
            src_ref=gathered.at[0, times], dst_ref=gathered.at[(3, 1)[d], times],
            send_sem=x_s.at[d, k], recv_sem=x_r.at[d, k],
            device_id=(g, (right, left)[d]), device_id_type=MESH,
        )

    def f_copy(k, d):
        times = pl.ds(pair_of(k), 2)
        return pltpu.make_async_remote_copy(
            src_ref=gathered.at[(3, 1)[d], times], dst_ref=gathered.at[2, times],
            send_sem=f_s.at[k], recv_sem=f_r.at[k],
            device_id=(g, (right, left)[d]), device_id_type=MESH,
        )

    def step(k, _):
        @pl.when(k < NPAIR)
        def _():
            for core in range(2):
                t = pair_of(k) + core

                @pl.when(t != g)
                def _():
                    arrival(t).wait_recv()

                @pl.when(t == g)
                def _():
                    own_copy.wait()

            x_copy(k, 0).start()
            x_copy(k, 1).start()

        @pl.when(k >= LAG)
        def _():
            m = k - LAG
            x_copy(m, 0).wait_recv()
            x_copy(m, 1).wait_recv()

            @pl.when(m % 2 == 0)
            def _():
                f_copy(m, 0).start()

            @pl.when(m % 2 == 1)
            def _():
                f_copy(m, 1).start()

        return 0

    lax.fori_loop(0, NPAIR + LAG, step, 0)

    def finish(k, _):
        x_copy(k, 0).wait_send()
        x_copy(k, 1).wait_send()
        f_copy(k, 0).wait_recv()
        f_copy(k, 0).wait_send()
        return 0

    lax.fori_loop(0, NPAIR, finish, 0)

    def sent(i, _):
        send_copy((g + i) % NT).wait_send()
        return 0

    lax.fori_loop(1, NT, sent, 0)
    flag_own.wait()
    for o in range(1, NB):
        flag_copy(o).wait_send()
        flag_copy(o).wait_recv()


def product_kernel(gathered, flags, out, wide, right_v, left_v, prod, out_v, out_sem):
    x = lax.axis_index("blk")

    codes = []
    for o in range(NB):
        same = flags[o, 1:2, :] == flags[0, 1:2, :]
        codes.append(jnp.where(same, flags[o, 0:1, :], 0).astype(F32))
    own_valid = jnp.broadcast_to(flags[0, 0:1, :].astype(F32) / NT, (LANES, LANES)).T
    row_masks = group_masks((1, LANES))
    keep = []
    for ha in range(4):
        code = pick(row_masks, [codes[(hb - ha) % 4] for hb in range(4)])
        keep.append(own_valid[ha * MB : (ha + 1) * MB] * code)

    for o in range(NB):
        for part in range(4):
            wide[pl.ds(part * 1024, 1024), :] = (
                gathered[o, pl.ds(part * 16, 16)].reshape(1024, LANES).astype(F32)
            )

        def relay(r, _):
            real = wide[pl.ds(2 * r, NT, stride=ROWS), :]
            imag = wide[pl.ds(2 * r + 1, NT, stride=ROWS), :]
            right_v[r, 0:NT, o * LANES : (o + 1) * LANES] = real.astype(BF16)
            right_v[r, NT : 2 * NT, o * LANES : (o + 1) * LANES] = imag.astype(BF16)
            if o == 0:
                left_v[r, 0:LANES] = jnp.concatenate([real, imag], axis=0).T.astype(BF16)
                left_v[r, LANES : 2 * LANES] = jnp.concatenate([imag, -real], axis=0).T.astype(BF16)
            return 0

        lax.fori_loop(0, NR, relay, 0, unroll=2)

    masks = group_masks((MB, LANES))

    def multiply(r, _):
        x_all = jnp.dot(left_v[r], right_v[r], preferred_element_type=F32)
        for c in range(2):
            for ha in range(4):
                rows = x_all[c * LANES + ha * MB : c * LANES + (ha + 1) * MB]
                values = []
                for hb in range(4):
                    o = (hb - ha) % 4
                    values.append(rows[:, o * LANES : (o + 1) * LANES])
                place = (r * 4 + (ha + NB - x) % 4) * MB
                prod[c, pl.ds(pl.multiple_of(place, MB), MB), :] = pick(masks, values) * keep[ha]
        return 0

    lax.fori_loop(0, NR, multiply, 0)

    lane = lax.broadcasted_iota(jnp.int32, (MB, LANES), 1) % 4
    delay_masks = [lane == d for d in range(4)]

    def out_copy(n):
        c, i8 = n // 4, n % 4
        return pltpu.make_async_copy(
            out_v.at[:, c, pl.ds(i8 * 8, 8)], out.at[:, c, pl.ds(i8 * 8, 8)], out_sem.at[n]
        )

    for c in range(2):
        for i8 in range(4):

            def turn(ii, _):
                i = i8 * 8 + ii
                flat = prod[c, pl.ds(i, LANES, stride=MB), :].T
                for p in range(NB):
                    values = [flat[((d + p) % 4) * MB : ((d + p) % 4 + 1) * MB] for d in range(4)]
                    out_v[p, c, i] = pick(delay_masks, values)
                return 0

            lax.fori_loop(0, 8, turn, 0, unroll=2)
            out_copy(c * 4 + i8).start()
    for n in range(8):
        out_copy(n).wait()


def local(visibility, block_group, member_valid):
    vis = visibility.reshape(NT * MB, 2 * CH)
    table = jnp.asarray(delay_table())
    dma = pltpu.SemaphoreType.DMA
    hbm_spec = pl.BlockSpec(memory_space=pltpu.HBM)
    vmem_spec = pl.BlockSpec(memory_space=pltpu.VMEM)
    gathered, flags = pl.pallas_call(
        exchange_kernel,
        name="exchange",
        out_shape=(
            jax.ShapeDtypeStruct((NB, NT, ROWS, LANES), BF16),
            jax.ShapeDtypeStruct((NB, 8, LANES), jnp.int32),
        ),
        in_specs=[hbm_spec] * 4,
        out_specs=(vmem_spec, vmem_spec),
        scratch_shapes=[
            pltpu.VMEM((NCHUNK, CHUNK * MB, 2 * CH), BF16),
            pltpu.VMEM((2 * DBAND, 2 * CH), BF16),
            pltpu.VMEM((1, MB), jnp.int32),
            pltpu.VMEM((1, 1), jnp.int32),
            pltpu.VMEM((2 * DBAND, CHUNK * MB), F32),
            pltpu.VMEM((NT, ROWS, LANES), BF16),
            pltpu.VMEM((8, LANES), jnp.int32),
            dma((NCHUNK,)), dma, dma, dma, dma, dma,
            dma((NT,)), dma((NT,)),
            dma((2, NPAIR)), dma((2, NPAIR)),
            dma((NPAIR,)), dma((NPAIR,)),
            dma((NB,)), dma((NB,)),
        ],
        compiler_params=pltpu.CompilerParams(
            collective_id=0, has_side_effects=True, vmem_limit_bytes=119 << 19
        ),
    )(vis, table, member_valid.reshape(1, MB), block_group.reshape(1, 1))
    result = pl.pallas_call(
        product_kernel,
        name="products",
        out_shape=jax.ShapeDtypeStruct((NB, 2, MB, MB, DBAND), F32),
        in_specs=[vmem_spec, vmem_spec],
        out_specs=hbm_spec,
        scratch_shapes=[
            pltpu.VMEM((NT * ROWS, LANES), F32),
            pltpu.VMEM((NR, 2 * NT, NB * LANES), BF16),
            pltpu.VMEM((NR, 2 * LANES, 2 * NT), BF16),
            pltpu.VMEM((2, DBAND * MB, LANES), F32),
            pltpu.VMEM((NB, 2, MB, MB, DBAND), F32),
            dma((8,)),
        ],
        compiler_params=pltpu.CompilerParams(vmem_limit_bytes=40 << 20),
    )(gathered, flags)
    return result[None, None]


def solution(mesh):
    in_specs = (P("grp", "blk", None, None, None), P("blk", "grp"), P("blk", "grp", None))
    out_specs = P("blk", "grp", None, None, None, None, None)
    return jax.shard_map(local, mesh=mesh, in_specs=in_specs, out_specs=out_specs, check_vma=False)
```

time: 175 us -> 83.5 us (0.48)
  Pallas kernels: 0 us -> 79.8 us
  blocking collectives: 55.7 us -> 0 us
  local copies, waits for them, and re-layouts: 40.6 us -> 2.9 us
  matrix products: 33.5 us -> 0 us
  waiting for transfers between devices: 23.1 us -> 0 us
  between operations: 14.1 us -> 0.67 us
  other arithmetic: 6.88 us -> 0 us
    pallas_call x0 -> x2, Pallas kernels: none -> 79.8 us  [the longest x1 59.4 us: local(): pl.pallas_call(exchange_kernel, name='exchange', out_shape=(jax.ShapeDtyp...]
    all_to_all x1 -> x0, blocking collectives: 41.7 us -> none  [local(): lax.all_to_all(local_spectra, 'grp', split_axis=2, concat_axis=0, tiled=T...]
    dot_general x5 -> x0, matrix products: 33.5 us -> none  [the longest x1 13.1 us: local(): jnp.dot(visibility, table, preferred_element_type=jnp.float32)]
    all_gather x1 -> x0, waiting for transfers between devices: 23 us -> none  [local(): lax.all_gather(spectra, 'blk', axis=1, tiled=True)]
    another operation x2 -> x0, local copies, waits for them, and re-layouts: 16.3 us -> none  [local(): stacked = jnp.stack([cross_real, cross_imag], axis=1)]
    all_gather x1 -> x0, local copies, waits for them, and re-layouts: 13 us -> none  [local(): lax.all_gather(spectra, 'blk', axis=1, tiled=True)]
    unnamed x1 -> x0, blocking collectives: 8.46 us -> none
    all_gather x1 -> x0, blocking collectives: 5.58 us -> none  [local(): lax.all_gather(flags_sent, 'blk', axis=0, tiled=True)]
  transfers between devices with their start and end apart: 1 -> 0, of which waited for: 1 -> 0; matrix products, arithmetic and copies ran while one was open for 6% -> 0% of each run, Pallas kernels for 0% -> 0%
where the time goes in v1:
time: 83.5 us; the launch traced here: 83.4 us
  Pallas kernels  79.8 us (96%)
  local copies, waits for them, and re-layouts  2.9 us (3%)
    pallas_call x1, Pallas kernels, local(): pl.pallas_call(exchange_kernel, name='exchange', out_shape=(jax.ShapeDtyp...  59.4 us
    pallas_call x1, Pallas kernels, local(): pl.pallas_call(product_kernel, name='products', out_shape=jax.ShapeDtypeS...  20.4 us
    unnamed x4, local copies, waits for them, and re-layouts  2.9 us

profile of v1, /device:TPU:1, one launch (start us, length us, event | category | flops | bytes accessed | tf_op | source)
XLA Modules:
  0.0 83.4 jit_solution(7037837384990442449)
XLA Ops:
  0.7 59.4 %exchange.1 = (bf16[4,64,64,128]{3,2,1,0:T(8,128)(2,1)}, s32[4,8,128]{2,1,0:T(8,128)}) custom-call(bf16[2048,2048]{1,0:T(8,128)(2,1)} %bitcast.3, bf16[256,2048]{1,0:T(8,128)(2,1)} %constant.2.clone.table, s32[1,32]{1,0:T(1,128)} %bitcast.4, s32[1,1]{1,0:T(1,128)S(6)} %copy.5.label), custom_call_target="tpu_custom_call" | custom-call | tf_op jit(solution)/shard_map/exchange/pallas_call | solution.py:329
  60.0 0.0 copy-start
  60.0 2.2 %copy-done = bf16[4,64,64,128]{3,2,1,0:T(8,128)(2,1)S(1)} copy-done((bf16[4,64,64,128]{3,2,1,0:T(8,128)(2,1)S(1)}, bf16[4,64,64,128]{3,2,1,0:T(8,128)(2,1)}, u32[]{:S(2)}) %copy-start) | copy-done | bytes 4194328
  62.2 0.0 copy-start.1
  62.2 0.7 copy-done.1
  62.9 20.4 %products.1 = f32[4,2,32,32,128]{4,3,2,1,0:T(8,128)} custom-call(bf16[4,64,64,128]{3,2,1,0:T(8,128)(2,1)S(1)} %copy-done, s32[4,8,128]{2,1,0:T(8,128)S(1)} %copy-done.1), custom_call_target="tpu_custom_call" | custom-call | tf_op jit(solution)/shard_map/products/pallas_call | solution.py:356
Async XLA Ops:
  60.0 2.2 %copy-start = (bf16[4,64,64,128]{3,2,1,0:T(8,128)(2,1)S(1)}, bf16[4,64,64,128]{3,2,1,0:T(8,128)(2,1)}, u32[]{:S(2)}) copy-start(bf16[4,64,64,128]{3,2,1,0:T(8,128)(2,1)} %get-tuple-element.7.gathered) | copy-start | bytes 12582916
  62.2 0.7 copy-start.1

commit v2 on v1

--- a/solution.py
+++ b/solution.py
@@ -25,8 +25,10 @@
 NR = DBAND // 4
 CHUNK = 8
 NCHUNK = NT // CHUNK
-NPAIR = NT // 2
+NCELL = NT // 2
 LAG = 8
+OTHER = 0
+STRIDE = 72
 
 
 def delay_table():
@@ -49,6 +51,10 @@
     return rows.astype(np.float32).astype(ml_dtypes.bfloat16)
 
 
+def entry_class(z):
+    return z - (z // 4) * (z - 4)
+
+
 def group_masks(shape):
     group = lax.broadcasted_iota(jnp.int32, shape, 1) // MB
     return [group == h for h in range(4)]
@@ -65,7 +71,7 @@
     vis, table, valid, label, gathered, flags,
     vis_v, table_v, valid_v, label_v, turned, send, own_flags,
     vis_sem, table_sem, valid_sem, label_sem, own_sem, flag_own_sem,
-    a_s, a_r, x_s, x_r, f_s, f_r, g_s, g_r,
+    present, a_s, a_r, x_s, x_r, f_s, f_r, g_s, g_r,
 ):
     g = lax.axis_index("grp")
     x = lax.axis_index("blk")
@@ -73,7 +79,7 @@
     right, left = (x + 1) % 4, (x + 3) % 4
 
     def chunk_of(k):
-        return ((y + k // 2) % 4) * 2 + (zh + k) % 2
+        return ((y + k) % 4) * 2 + (zh + k // 4) % 2
 
     def vis_copy(k):
         rows = pl.ds(pl.multiple_of(chunk_of(k) * CHUNK * MB, CHUNK * MB), CHUNK * MB)
@@ -90,13 +96,23 @@
 
     barrier = pltpu.get_barrier_semaphore()
 
-    def greet(i, _):
-        pl.semaphore_signal(barrier, inc=1, device_id=((g + i) % NT, x), device_id_type=MESH)
-        return 0
-
-    lax.fori_loop(1, NT, greet, 0)
+    mine = entry_class(z)
+
+    def plane(pz, sem):
+        for py in range(NY):
+            for core in range(2):
+                t = py * 16 + pz * 2 + core
+
+                @pl.when(t != g)
+                def _():
+                    pl.semaphore_signal(sem, inc=1, device_id=(t, x), device_id_type=MESH)
+
+    lax.fori_loop(mine, NZ, lambda pz, _: (plane(pz, barrier), 0)[1], 0)
     for o in range(1, NB):
         pl.semaphore_signal(barrier, inc=1, device_id=(g, (x + o) % NB), device_id_type=MESH)
+    last = mine + 1 + (z // 4) * 3
+    pl.semaphore_wait(barrier, last * 8 - 1 + NB - 1)
+    lax.fori_loop(0, mine, lambda pz, _: (plane(pz, present.at[z]), 0)[1], 0)
 
     valid_copy.wait()
     label_copy.wait()
@@ -129,6 +145,17 @@
             send_sem=g_s.at[o], recv_sem=g_r.at[o],
             device_id=(g, (x + NB - o) % NB), device_id_type=MESH,
         )
+
+    def send_to(t0, new_plane):
+        @pl.when(new_plane & (entry_class((t0 // 2) % 8) > mine))
+        def _():
+            pl.semaphore_wait(present.at[(t0 // 2) % 8], 8)
+
+        for core in range(2):
+
+            @pl.when(t0 + core != g)
+            def _():
+                send_copy(t0 + core).start()
 
     def transform(k, _):
         vis_copy(k).wait()
@@ -152,27 +179,23 @@
 
         @pl.when(k == 0)
         def _():
-            pl.semaphore_wait(barrier, NT - 1 + NB - 1)
             own_copy.start()
             flag_own.start()
             for o in range(1, NB):
                 flag_copy(o).start()
 
-        for dz in range(4):
-            for core in range(2):
-                t = chunk * CHUNK + ((zl + dz) % 4) * 2 + core
-
-                @pl.when(t != g)
-                def _():
-                    send_copy(t).start()
+        @pl.when(k < 4)
+        def _():
+            for dz in range(4):
+                send_to(chunk * CHUNK + ((zl + dz) % 4) * 2, k == 0)
 
         return 0
 
     lax.fori_loop(0, NCHUNK, transform, 0)
 
     def pair_of(k):
-        step, dz = k // 4, k % 4
-        return ((y + 4 - step // 2) % 4) * 16 + ((zh + step) % 2) * 8 + ((zl + 4 - dz) % 4) * 2
+        dy, dz = (k // 4) % 4, k % 4
+        return ((y + 4 - dy) % 4) * 16 + ((zh + k // 16) % 2) * 8 + ((zl + 4 - dz) % 4) * 2
 
     def x_copy(k, d):
         times = pl.ds(pair_of(k), 2)
@@ -191,7 +214,12 @@
         )
 
     def step(k, _):
-        @pl.when(k < NPAIR)
+        @pl.when((k >= OTHER) & (k < OTHER + 16))
+        def _():
+            n = k - OTHER
+            send_to(chunk_of(4 + n // 4) * CHUNK + ((zl + n % 4) % 4) * 2, n < 4)
+
+        @pl.when(k < NCELL)
         def _():
             for core in range(2):
                 t = pair_of(k) + core
@@ -223,7 +251,7 @@
 
         return 0
 
-    lax.fori_loop(0, NPAIR + LAG, step, 0)
+    lax.fori_loop(0, NCELL + LAG, step, 0)
 
     def finish(k, _):
         x_copy(k, 0).wait_send()
@@ -232,7 +260,7 @@
         f_copy(k, 0).wait_send()
         return 0
 
-    lax.fori_loop(0, NPAIR, finish, 0)
+    lax.fori_loop(0, NCELL, finish, 0)
 
     def sent(i, _):
         send_copy((g + i) % NT).wait_send()
@@ -260,14 +288,16 @@
         keep.append(own_valid[ha * MB : (ha + 1) * MB] * code)
 
     for o in range(NB):
-        for part in range(4):
-            wide[pl.ds(part * 1024, 1024), :] = (
-                gathered[o, pl.ds(part * 16, 16)].reshape(1024, LANES).astype(F32)
-            )
+        def widen(t, _):
+            rows = pl.ds(pl.multiple_of(t * STRIDE, 8), ROWS)
+            wide[rows, :] = gathered[o, t].astype(F32)
+            return 0
+
+        lax.fori_loop(0, NT, widen, 0, unroll=8)
 
         def relay(r, _):
-            real = wide[pl.ds(2 * r, NT, stride=ROWS), :]
-            imag = wide[pl.ds(2 * r + 1, NT, stride=ROWS), :]
+            real = wide[pl.ds(2 * r, NT, stride=STRIDE), :]
+            imag = wide[pl.ds(2 * r + 1, NT, stride=STRIDE), :]
             right_v[r, 0:NT, o * LANES : (o + 1) * LANES] = real.astype(BF16)
             right_v[r, NT : 2 * NT, o * LANES : (o + 1) * LANES] = imag.astype(BF16)
             if o == 0:
@@ -275,7 +305,7 @@
                 left_v[r, LANES : 2 * LANES] = jnp.concatenate([imag, -real], axis=0).T.astype(BF16)
             return 0
 
-        lax.fori_loop(0, NR, relay, 0, unroll=2)
+        lax.fori_loop(0, NR, relay, 0, unroll=8)
 
     masks = group_masks((MB, LANES))
 
@@ -292,7 +322,7 @@
                 prod[c, pl.ds(pl.multiple_of(place, MB), MB), :] = pick(masks, values) * keep[ha]
         return 0
 
-    lax.fori_loop(0, NR, multiply, 0)
+    lax.fori_loop(0, NR, multiply, 0, unroll=8)
 
     lane = lax.broadcasted_iota(jnp.int32, (MB, LANES), 1) % 4
     delay_masks = [lane == d for d in range(4)]
@@ -314,7 +344,7 @@
                     out_v[p, c, i] = pick(delay_masks, values)
                 return 0
 
-            lax.fori_loop(0, 8, turn, 0, unroll=2)
+            lax.fori_loop(0, 8, turn, 0, unroll=8)
             out_copy(c * 4 + i8).start()
     for n in range(8):
         out_copy(n).wait()
@@ -344,9 +374,10 @@
             pltpu.VMEM((NT, ROWS, LANES), BF16),
             pltpu.VMEM((8, LANES), jnp.int32),
             dma((NCHUNK,)), dma, dma, dma, dma, dma,
+            pltpu.SemaphoreType.REGULAR((NZ,)),
             dma((NT,)), dma((NT,)),
-            dma((2, NPAIR)), dma((2, NPAIR)),
-            dma((NPAIR,)), dma((NPAIR,)),
+            dma((2, NCELL)), dma((2, NCELL)),
+            dma((NCELL,)), dma((NCELL,)),
             dma((NB,)), dma((NB,)),
         ],
         compiler_params=pltpu.CompilerParams(
@@ -360,7 +391,7 @@
         in_specs=[vmem_spec, vmem_spec],
         out_specs=hbm_spec,
         scratch_shapes=[
-            pltpu.VMEM((NT * ROWS, LANES), F32),
+            pltpu.VMEM((NT * STRIDE, LANES), F32),
             pltpu.VMEM((NR, 2 * NT, NB * LANES), BF16),
             pltpu.VMEM((NR, 2 * LANES, 2 * NT), BF16),
             pltpu.VMEM((2, DBAND * MB, LANES), F32),

time: 83.5 us -> 72.5 us (0.87)
  Pallas kernels: 79.8 us -> 68.7 us
    pallas_call x1, Pallas kernels: 20.4 us -> 9.05 us  [local(): pl.pallas_call(product_kernel, name='products', out_shape=jax.ShapeDtypeS...]
where the time goes in v2:
time: 72.5 us; the launch traced here: 72.3 us
  Pallas kernels  68.7 us (95%)
  local copies, waits for them, and re-layouts  2.9 us (4%)
    pallas_call x1, Pallas kernels, local(): pl.pallas_call(exchange_kernel, name='exchange', out_shape=(jax.ShapeDtyp...  59.7 us
    pallas_call x1, Pallas kernels, local(): pl.pallas_call(product_kernel, name='products', out_shape=jax.ShapeDtypeS...  9.05 us
    unnamed x4, local copies, waits for them, and re-layouts  2.9 us

profile of v2, /device:TPU:1, one launch (start us, length us, event | category | flops | bytes accessed | tf_op | source)
XLA Modules:
  0.0 72.3 jit_solution(3544139959488441373)
XLA Ops:
  0.7 59.7 %exchange.1 = (bf16[4,64,64,128]{3,2,1,0:T(8,128)(2,1)}, s32[4,8,128]{2,1,0:T(8,128)}) custom-call(bf16[2048,2048]{1,0:T(8,128)(2,1)} %bitcast.3, bf16[256,2048]{1,0:T(8,128)(2,1)} %constant.2.clone.table, s32[1,32]{1,0:T(1,128)} %bitcast.4, s32[1,1]{1,0:T(1,128)S(6)} %copy.5.label), custom_call_target="tpu_custom_call" | custom-call | tf_op jit(solution)/shard_map/exchange/pallas_call | solution.py:359
  60.4 0.0 copy-start
  60.4 2.2 %copy-done = bf16[4,64,64,128]{3,2,1,0:T(8,128)(2,1)S(1)} copy-done((bf16[4,64,64,128]{3,2,1,0:T(8,128)(2,1)S(1)}, bf16[4,64,64,128]{3,2,1,0:T(8,128)(2,1)}, u32[]{:S(2)}) %copy-start) | copy-done | bytes 4194328
  62.5 0.0 copy-start.1
  62.5 0.7 copy-done.1
  63.3 9.0 %products.1 = f32[4,2,32,32,128]{4,3,2,1,0:T(8,128)} custom-call(bf16[4,64,64,128]{3,2,1,0:T(8,128)(2,1)S(1)} %copy-done, s32[4,8,128]{2,1,0:T(8,128)S(1)} %copy-done.1), custom_call_target="tpu_custom_call" | custom-call | tf_op jit(solution)/shard_map/products/pallas_call | solution.py:387
Async XLA Ops:
  60.4 2.2 %copy-start = (bf16[4,64,64,128]{3,2,1,0:T(8,128)(2,1)S(1)}, bf16[4,64,64,128]{3,2,1,0:T(8,128)(2,1)}, u32[]{:S(2)}) copy-start(bf16[4,64,64,128]{3,2,1,0:T(8,128)(2,1)} %get-tuple-element.7.gathered) | copy-start | bytes 12582916
  62.5 0.7 copy-start.1

commit v3 on v2

--- a/solution.py
+++ b/solution.py
@@ -27,7 +27,9 @@
 NCHUNK = NT // CHUNK
 NCELL = NT // 2
 LAG = 8
-OTHER = 0
+DELAY = 3
+EXCHANGE_VMEM = 48 << 20
+TURN_VMEM = 16 << 20
 STRIDE = 72
 
 
@@ -68,8 +70,8 @@
 
 
 def exchange_kernel(
-    vis, table, valid, label, gathered, flags,
-    vis_v, table_v, valid_v, label_v, turned, send, own_flags,
+    vis, table, valid, label, prod,
+    vis_v, table_v, valid_v, label_v, turned, send, own_flags, flags, gathered, wide, right_v, left_v,
     vis_sem, table_sem, valid_sem, label_sem, own_sem, flag_own_sem,
     present, a_s, a_r, x_s, x_r, f_s, f_r, g_s, g_r,
 ):
@@ -184,14 +186,14 @@
             for o in range(1, NB):
                 flag_copy(o).start()
 
-        @pl.when(k < 4)
+        for dz in range(4):
+            send_to(chunk * CHUNK + ((zl + dz) % 4) * 2, k % 4 == 0)
+
+        @pl.when(k >= DELAY)
         def _():
-            for dz in range(4):
-                send_to(chunk * CHUNK + ((zl + dz) % 4) * 2, k == 0)
+            lax.fori_loop(4 * (k - DELAY), 4 * (k - DELAY + 1), step, 0)
 
         return 0
-
-    lax.fori_loop(0, NCHUNK, transform, 0)
 
     def pair_of(k):
         dy, dz = (k // 4) % 4, k % 4
@@ -214,11 +216,6 @@
         )
 
     def step(k, _):
-        @pl.when((k >= OTHER) & (k < OTHER + 16))
-        def _():
-            n = k - OTHER
-            send_to(chunk_of(4 + n // 4) * CHUNK + ((zl + n % 4) % 4) * 2, n < 4)
-
         @pl.when(k < NCELL)
         def _():
             for core in range(2):
@@ -251,7 +248,53 @@
 
         return 0
 
-    lax.fori_loop(0, NCELL + LAG, step, 0)
+    lax.fori_loop(0, NCHUNK, transform, 0)
+    lax.fori_loop(4 * (NCHUNK - DELAY), NCELL, step, 0)
+
+    flag_own.wait()
+    for o in range(1, NB):
+        flag_copy(o).wait_recv()
+    keep = keep_masks(flags)
+    place_masks = group_masks((MB, LANES))
+
+    def products(o):
+        def widen(t, _):
+            rows = pl.ds(pl.multiple_of(t * STRIDE, 8), ROWS)
+            wide[rows, :] = gathered[o, t].astype(F32)
+            return 0
+
+        lax.fori_loop(0, NT, widen, 0, unroll=8)
+
+        def relay(r, _):
+            real = wide[pl.ds(2 * r, NT, stride=STRIDE), :]
+            imag = wide[pl.ds(2 * r + 1, NT, stride=STRIDE), :]
+            right_v[r, 0:NT] = real.astype(BF16)
+            right_v[r, NT : 2 * NT] = imag.astype(BF16)
+            if o == 0:
+                left_v[r, 0:LANES] = jnp.concatenate([real, imag], axis=0).T.astype(BF16)
+                left_v[r, LANES : 2 * LANES] = jnp.concatenate([imag, -real], axis=0).T.astype(BF16)
+            return 0
+
+        lax.fori_loop(0, NR, relay, 0, unroll=8)
+
+        def multiply(r, _):
+            x_all = jnp.dot(left_v[r], right_v[r], preferred_element_type=F32)
+            for c in range(2):
+                for ha in range(4):
+                    rows = x_all[c * LANES + ha * MB : c * LANES + (ha + 1) * MB] * keep[ha]
+                    place = (r * 4 + (ha + NB - x) % 4) * MB
+                    pltpu.store(
+                        prod.at[c, pl.ds(pl.multiple_of(place, MB), MB), :],
+                        rows, mask=place_masks[(ha + o) % 4],
+                    )
+            return 0
+
+        lax.fori_loop(0, NR, multiply, 0, unroll=8)
+
+    products(0)
+    lax.fori_loop(NCELL, NCELL + LAG, step, 0)
+    products(1)
+    products(3)
 
     def finish(k, _):
         x_copy(k, 0).wait_send()
@@ -261,21 +304,18 @@
         return 0
 
     lax.fori_loop(0, NCELL, finish, 0)
+    products(2)
 
     def sent(i, _):
         send_copy((g + i) % NT).wait_send()
         return 0
 
     lax.fori_loop(1, NT, sent, 0)
-    flag_own.wait()
     for o in range(1, NB):
         flag_copy(o).wait_send()
-        flag_copy(o).wait_recv()
-
-
-def product_kernel(gathered, flags, out, wide, right_v, left_v, prod, out_v, out_sem):
-    x = lax.axis_index("blk")
-
+
+
+def keep_masks(flags):
     codes = []
     for o in range(NB):
         same = flags[o, 1:2, :] == flags[0, 1:2, :]
@@ -286,44 +326,10 @@
     for ha in range(4):
         code = pick(row_masks, [codes[(hb - ha) % 4] for hb in range(4)])
         keep.append(own_valid[ha * MB : (ha + 1) * MB] * code)
-
-    for o in range(NB):
-        def widen(t, _):
-            rows = pl.ds(pl.multiple_of(t * STRIDE, 8), ROWS)
-            wide[rows, :] = gathered[o, t].astype(F32)
-            return 0
-
-        lax.fori_loop(0, NT, widen, 0, unroll=8)
-
-        def relay(r, _):
-            real = wide[pl.ds(2 * r, NT, stride=STRIDE), :]
-            imag = wide[pl.ds(2 * r + 1, NT, stride=STRIDE), :]
-            right_v[r, 0:NT, o * LANES : (o + 1) * LANES] = real.astype(BF16)
-            right_v[r, NT : 2 * NT, o * LANES : (o + 1) * LANES] = imag.astype(BF16)
-            if o == 0:
-                left_v[r, 0:LANES] = jnp.concatenate([real, imag], axis=0).T.astype(BF16)
-                left_v[r, LANES : 2 * LANES] = jnp.concatenate([imag, -real], axis=0).T.astype(BF16)
-            return 0
-
-        lax.fori_loop(0, NR, relay, 0, unroll=8)
-
-    masks = group_masks((MB, LANES))
-
-    def multiply(r, _):
-        x_all = jnp.dot(left_v[r], right_v[r], preferred_element_type=F32)
-        for c in range(2):
-            for ha in range(4):
-                rows = x_all[c * LANES + ha * MB : c * LANES + (ha + 1) * MB]
-                values = []
-                for hb in range(4):
-                    o = (hb - ha) % 4
-                    values.append(rows[:, o * LANES : (o + 1) * LANES])
-                place = (r * 4 + (ha + NB - x) % 4) * MB
-                prod[c, pl.ds(pl.multiple_of(place, MB), MB), :] = pick(masks, values) * keep[ha]
-        return 0
-
-    lax.fori_loop(0, NR, multiply, 0, unroll=8)
-
+    return keep
+
+
+def turn_kernel(prod, out, out_v, out_sem):
     lane = lax.broadcasted_iota(jnp.int32, (MB, LANES), 1) % 4
     delay_masks = [lane == d for d in range(4)]
 
@@ -356,15 +362,12 @@
     dma = pltpu.SemaphoreType.DMA
     hbm_spec = pl.BlockSpec(memory_space=pltpu.HBM)
     vmem_spec = pl.BlockSpec(memory_space=pltpu.VMEM)
-    gathered, flags = pl.pallas_call(
+    prod = pl.pallas_call(
         exchange_kernel,
         name="exchange",
-        out_shape=(
-            jax.ShapeDtypeStruct((NB, NT, ROWS, LANES), BF16),
-            jax.ShapeDtypeStruct((NB, 8, LANES), jnp.int32),
-        ),
+        out_shape=jax.ShapeDtypeStruct((2, DBAND * MB, LANES), F32),
         in_specs=[hbm_spec] * 4,
-        out_specs=(vmem_spec, vmem_spec),
+        out_specs=vmem_spec,
         scratch_shapes=[
             pltpu.VMEM((NCHUNK, CHUNK * MB, 2 * CH), BF16),
             pltpu.VMEM((2 * DBAND, 2 * CH), BF16),
@@ -373,6 +376,11 @@
             pltpu.VMEM((2 * DBAND, CHUNK * MB), F32),
             pltpu.VMEM((NT, ROWS, LANES), BF16),
             pltpu.VMEM((8, LANES), jnp.int32),
+            pltpu.VMEM((NB, 8, LANES), jnp.int32),
+            pltpu.VMEM((NB, NT, ROWS, LANES), BF16),
+            pltpu.VMEM((NT * STRIDE, LANES), F32),
+            pltpu.VMEM((NR, 2 * NT, LANES), BF16),
+            pltpu.VMEM((NR, 2 * LANES, 2 * NT), BF16),
             dma((NCHUNK,)), dma, dma, dma, dma, dma,
             pltpu.SemaphoreType.REGULAR((NZ,)),
             dma((NT,)), dma((NT,)),
@@ -381,25 +389,24 @@
             dma((NB,)), dma((NB,)),
         ],
         compiler_params=pltpu.CompilerParams(
-            collective_id=0, has_side_effects=True, vmem_limit_bytes=119 << 19
+            collective_id=0, has_side_effects=True, vmem_limit_bytes=EXCHANGE_VMEM
         ),
-    )(vis, table, member_valid.reshape(1, MB), block_group.reshape(1, 1))
+    )(
+        *(
+            pltpu.with_memory_space_constraint(a, pltpu.HBM)
+            for a in (vis, table, member_valid.reshape(1, MB))
+        ),
+        block_group.reshape(1, 1),
+    )
     result = pl.pallas_call(
-        product_kernel,
-        name="products",
+        turn_kernel,
+        name="turn",
         out_shape=jax.ShapeDtypeStruct((NB, 2, MB, MB, DBAND), F32),
-        in_specs=[vmem_spec, vmem_spec],
+        in_specs=[vmem_spec],
         out_specs=hbm_spec,
-        scratch_shapes=[
-            pltpu.VMEM((NT * STRIDE, LANES), F32),
-            pltpu.VMEM((NR, 2 * NT, NB * LANES), BF16),
-            pltpu.VMEM((NR, 2 * LANES, 2 * NT), BF16),
-            pltpu.VMEM((2, DBAND * MB, LANES), F32),
-            pltpu.VMEM((NB, 2, MB, MB, DBAND), F32),
-            dma((8,)),
-        ],
-        compiler_params=pltpu.CompilerParams(vmem_limit_bytes=40 << 20),
-    )(gathered, flags)
+        scratch_shapes=[pltpu.VMEM((NB, 2, MB, MB, DBAND), F32), dma((8,))],
+        compiler_params=pltpu.CompilerParams(vmem_limit_bytes=TURN_VMEM),
+    )(prod)
     return result[None, None]
 
 

time: 72.5 us -> 62.8 us (0.87)
  Pallas kernels: 68.7 us -> 61.9 us
  local copies, waits for them, and re-layouts: 2.9 us -> 0 us
    pallas_call x2, Pallas kernels: 68.7 us -> 61.9 us  [the longest x1 58.7 us: local(): pl.pallas_call(exchange_kernel, name='exchange', out_shape=jax.ShapeDtype...]
    unnamed x4 -> x0, local copies, waits for them, and re-layouts: 2.9 us -> none
where the time goes in v3:
time: 62.8 us; the launch traced here: 62.6 us
  Pallas kernels  61.9 us (99%)
  between operations  0.66 us (1%)
    pallas_call x1, Pallas kernels, local(): pl.pallas_call(exchange_kernel, name='exchange', out_shape=jax.ShapeDtype...  58.7 us
    pallas_call x1, Pallas kernels, local(): pl.pallas_call(turn_kernel, name='turn', out_shape=jax.ShapeDtypeStruct((...  3.29 us

profile of v3, /device:TPU:1, one launch (start us, length us, event | category | flops | bytes accessed | tf_op | source)
XLA Modules:
  0.0 62.6 jit_solution(16010642503192371748)
XLA Ops:
  0.7 58.7 %exchange.1.prod = f32[2,4096,128]{2,1,0:T(8,128)S(1)} custom-call(bf16[2048,2048]{1,0:T(8,128)(2,1)} %bitcast.3, bf16[256,2048]{1,0:T(8,128)(2,1)} %constant.2.clone.table, s32[1,32]{1,0:T(1,128)} %bitcast.4, s32[1,1]{1,0:T(1,128)S(6)} %copy.5.label), custom_call_target="tpu_custom_call" | custom-call | tf_op jit(solution)/shard_map/exchange/pallas_call | solution.py:365
  59.3 3.3 %turn.1 = f32[4,2,32,32,128]{4,3,2,1,0:T(8,128)} custom-call(f32[2,4096,128]{2,1,0:T(8,128)S(1)} %exchange.1.prod), custom_call_target="tpu_custom_call" | custom-call | tf_op jit(solution)/shard_map/turn/pallas_call | solution.py:401

commit v4 on v3

--- a/solution.py
+++ b/solution.py
@@ -126,14 +126,14 @@
     def send_copy(t):
         return pltpu.make_async_remote_copy(
             src_ref=send.at[t], dst_ref=gathered.at[0, g],
-            send_sem=a_s.at[t], recv_sem=a_r.at[g],
+            send_sem=a_s, recv_sem=a_r.at[g],
             device_id=(t, x), device_id_type=MESH,
         )
 
     def arrival(t):
         return pltpu.make_async_remote_copy(
             src_ref=send.at[t], dst_ref=gathered.at[0, t],
-            send_sem=a_s.at[t], recv_sem=a_r.at[t],
+            send_sem=a_s, recv_sem=a_r.at[t],
             device_id=(t, x), device_id_type=MESH,
         )
 
@@ -203,7 +203,7 @@
         times = pl.ds(pair_of(k), 2)
         return pltpu.make_async_remote_copy(
             src_ref=gathered.at[0, times], dst_ref=gathered.at[(3, 1)[d], times],
-            send_sem=x_s.at[d, k], recv_sem=x_r.at[d, k],
+            send_sem=x_s.at[d], recv_sem=x_r.at[d, k],
             device_id=(g, (right, left)[d]), device_id_type=MESH,
         )
 
@@ -211,7 +211,7 @@
         times = pl.ds(pair_of(k), 2)
         return pltpu.make_async_remote_copy(
             src_ref=gathered.at[(3, 1)[d], times], dst_ref=gathered.at[2, times],
-            send_sem=f_s.at[k], recv_sem=f_r.at[k],
+            send_sem=f_s, recv_sem=f_r,
             device_id=(g, (right, left)[d]), device_id_type=MESH,
         )
 
@@ -257,60 +257,72 @@
     keep = keep_masks(flags)
     place_masks = group_masks((MB, LANES))
 
-    def products(o):
-        def widen(t, _):
-            rows = pl.ds(pl.multiple_of(t * STRIDE, 8), ROWS)
-            wide[rows, :] = gathered[o, t].astype(F32)
-            return 0
-
-        lax.fori_loop(0, NT, widen, 0, unroll=8)
-
-        def relay(r, _):
-            real = wide[pl.ds(2 * r, NT, stride=STRIDE), :]
-            imag = wide[pl.ds(2 * r + 1, NT, stride=STRIDE), :]
-            right_v[r, 0:NT] = real.astype(BF16)
-            right_v[r, NT : 2 * NT] = imag.astype(BF16)
-            if o == 0:
-                left_v[r, 0:LANES] = jnp.concatenate([real, imag], axis=0).T.astype(BF16)
-                left_v[r, LANES : 2 * LANES] = jnp.concatenate([imag, -real], axis=0).T.astype(BF16)
-            return 0
-
-        lax.fori_loop(0, NR, relay, 0, unroll=8)
+    def products(slots):
+        for n, o in enumerate(slots):
+
+            def widen(t, _):
+                rows = pl.ds(pl.multiple_of(t * STRIDE, 8), ROWS)
+                wide[rows, :] = gathered[o, t].astype(F32)
+                return 0
+
+            lax.fori_loop(0, NT, widen, 0, unroll=8)
+
+            def relay(r, _):
+                real = wide[pl.ds(2 * r, NT, stride=STRIDE), :]
+                imag = wide[pl.ds(2 * r + 1, NT, stride=STRIDE), :]
+                lanes = slice(n * LANES, (n + 1) * LANES)
+                right_v[r, 0:NT, lanes] = real.astype(BF16)
+                right_v[r, NT : 2 * NT, lanes] = imag.astype(BF16)
+                if o == 0:
+                    left_v[r, 0:LANES] = jnp.concatenate([real, imag], axis=0).T.astype(BF16)
+                    left_v[r, LANES : 2 * LANES] = (
+                        jnp.concatenate([imag, -real], axis=0).T.astype(BF16)
+                    )
+                return 0
+
+            lax.fori_loop(0, NR, relay, 0, unroll=8)
 
         def multiply(r, _):
-            x_all = jnp.dot(left_v[r], right_v[r], preferred_element_type=F32)
+            x_all = jnp.dot(
+                left_v[r], right_v[r, :, 0 : len(slots) * LANES], preferred_element_type=F32
+            )
             for c in range(2):
                 for ha in range(4):
-                    rows = x_all[c * LANES + ha * MB : c * LANES + (ha + 1) * MB] * keep[ha]
+                    rows = x_all[c * LANES + ha * MB : c * LANES + (ha + 1) * MB]
+                    mask = place_masks[(ha + slots[0]) % 4]
+                    value = rows[:, 0:LANES]
+                    if len(slots) == 2:
+                        value = jnp.where(mask, value, rows[:, LANES : 2 * LANES])
+                        mask = mask | place_masks[(ha + slots[1]) % 4]
                     place = (r * 4 + (ha + NB - x) % 4) * MB
                     pltpu.store(
                         prod.at[c, pl.ds(pl.multiple_of(place, MB), MB), :],
-                        rows, mask=place_masks[(ha + o) % 4],
+                        value * keep[ha], mask=mask,
                     )
             return 0
 
         lax.fori_loop(0, NR, multiply, 0, unroll=8)
 
-    products(0)
+    products((0,))
     lax.fori_loop(NCELL, NCELL + LAG, step, 0)
-    products(1)
-    products(3)
-
-    def finish(k, _):
-        x_copy(k, 0).wait_send()
-        x_copy(k, 1).wait_send()
-        f_copy(k, 0).wait_recv()
-        f_copy(k, 0).wait_send()
-        return 0
-
-    lax.fori_loop(0, NCELL, finish, 0)
-    products(2)
-
-    def sent(i, _):
-        send_copy((g + i) % NT).wait_send()
-        return 0
-
-    lax.fori_loop(1, NT, sent, 0)
+    products((1, 3))
+
+    def whole(slot, d, sent, received):
+        return pltpu.make_async_remote_copy(
+            src_ref=gathered.at[0], dst_ref=gathered.at[slot], send_sem=sent, recv_sem=received,
+            device_id=(g, (right, left)[d]), device_id_type=MESH,
+        )
+
+    forwards = whole(2, 0, f_s, f_r)
+    forwards.wait_recv()
+    products((2,))
+    forwards.wait_send()
+    for d in range(2):
+        whole((3, 1)[d], d, x_s.at[d], x_r.at[d, 0]).wait_send()
+    pltpu.make_async_remote_copy(
+        src_ref=send.at[pl.ds(0, NT - 1)], dst_ref=gathered.at[0, pl.ds(0, NT - 1)],
+        send_sem=a_s, recv_sem=a_r.at[0], device_id=(g, right), device_id_type=MESH,
+    ).wait_send()
     for o in range(1, NB):
         flag_copy(o).wait_send()
 
@@ -379,13 +391,13 @@
             pltpu.VMEM((NB, 8, LANES), jnp.int32),
             pltpu.VMEM((NB, NT, ROWS, LANES), BF16),
             pltpu.VMEM((NT * STRIDE, LANES), F32),
-            pltpu.VMEM((NR, 2 * NT, LANES), BF16),
+            pltpu.VMEM((NR, 2 * NT, 2 * LANES), BF16),
             pltpu.VMEM((NR, 2 * LANES, 2 * NT), BF16),
             dma((NCHUNK,)), dma, dma, dma, dma, dma,
             pltpu.SemaphoreType.REGULAR((NZ,)),
-            dma((NT,)), dma((NT,)),
-            dma((2, NCELL)), dma((2, NCELL)),
-            dma((NCELL,)), dma((NCELL,)),
+            dma, dma((NT,)),
+            dma((2,)), dma((2, NCELL)),
+            dma, dma,
             dma((NB,)), dma((NB,)),
         ],
         compiler_params=pltpu.CompilerParams(

time: 62.8 us -> 60.1 us (0.957)
  Pallas kernels: 61.9 us -> 58.7 us
    pallas_call x1, Pallas kernels: 58.7 us -> 55.5 us  [local(): pl.pallas_call(exchange_kernel, name='exchange', out_shape=jax.ShapeDtype...]
where the time goes in v4:
time: 60.1 us; the launch traced here: 59.4 us
  Pallas kernels  58.7 us (98%)
  between operations  0.66 us (1%)
    pallas_call x1, Pallas kernels, local(): pl.pallas_call(exchange_kernel, name='exchange', out_shape=jax.ShapeDtype...  55.5 us
    pallas_call x1, Pallas kernels, local(): pl.pallas_call(turn_kernel, name='turn', out_shape=jax.ShapeDtypeStruct((...  3.29 us

profile of v4, /device:TPU:1, one launch (start us, length us, event | category | flops | bytes accessed | tf_op | source)
XLA Modules:
  0.0 59.4 jit_solution(1719654144889811893)
XLA Ops:
  0.7 55.5 %exchange.1.prod = f32[2,4096,128]{2,1,0:T(8,128)S(1)} custom-call(bf16[2048,2048]{1,0:T(8,128)(2,1)} %bitcast.3, bf16[256,2048]{1,0:T(8,128)(2,1)} %constant.2.clone.table, s32[1,32]{1,0:T(1,128)} %bitcast.4, s32[1,1]{1,0:T(1,128)S(6)} %copy.5.label), custom_call_target="tpu_custom_call" | custom-call | tf_op jit(solution)/shard_map/exchange/pallas_call | solution.py:377
  56.1 3.3 %turn.1 = f32[4,2,32,32,128]{4,3,2,1,0:T(8,128)} custom-call(f32[2,4096,128]{2,1,0:T(8,128)S(1)} %exchange.1.prod), custom_call_target="tpu_custom_call" | custom-call | tf_op jit(solution)/shard_map/turn/pallas_call | solution.py:413

commit v5 on v4

--- a/solution.py
+++ b/solution.py
@@ -30,7 +30,7 @@
 DELAY = 3
 EXCHANGE_VMEM = 48 << 20
 TURN_VMEM = 16 << 20
-STRIDE = 72
+STRIDE = 68
 
 
 def delay_table():
@@ -260,12 +260,8 @@
     def products(slots):
         for n, o in enumerate(slots):
 
-            def widen(t, _):
-                rows = pl.ds(pl.multiple_of(t * STRIDE, 8), ROWS)
-                wide[rows, :] = gathered[o, t].astype(F32)
-                return 0
-
-            lax.fori_loop(0, NT, widen, 0, unroll=8)
+            for t in range(NT):
+                wide[t * STRIDE : t * STRIDE + ROWS, :] = gathered[o, t].astype(F32)
 
             def relay(r, _):
                 real = wide[pl.ds(2 * r, NT, stride=STRIDE), :]

time: 60.1 us -> 59.8 us (level)
  no operation moved by 1% of the time
where the time goes in v5:
time: 59.8 us; the launch traced here: 59.1 us
  Pallas kernels  58.4 us (98%)
  between operations  0.66 us (1%)
    pallas_call x1, Pallas kernels, local(): pl.pallas_call(exchange_kernel, name='exchange', out_shape=jax.ShapeDtype...  55.1 us
    pallas_call x1, Pallas kernels, local(): pl.pallas_call(turn_kernel, name='turn', out_shape=jax.ShapeDtypeStruct((...  3.29 us

profile of v5, /device:TPU:1, one launch (start us, length us, event | category | flops | bytes accessed | tf_op | source)
XLA Modules:
  0.0 59.1 jit_solution(1138215171646578103)
XLA Ops:
  0.7 55.1 %exchange.1.prod = f32[2,4096,128]{2,1,0:T(8,128)S(1)} custom-call(bf16[2048,2048]{1,0:T(8,128)(2,1)} %bitcast.3, bf16[256,2048]{1,0:T(8,128)(2,1)} %constant.2.clone.table, s32[1,32]{1,0:T(1,128)} %bitcast.4, s32[1,1]{1,0:T(1,128)S(6)} %copy.5.label), custom_call_target="tpu_custom_call" | custom-call | tf_op jit(solution)/shard_map/exchange/pallas_call | solution.py:373
  55.8 3.3 %turn.1 = f32[4,2,32,32,128]{4,3,2,1,0:T(8,128)} custom-call(f32[2,4096,128]{2,1,0:T(8,128)S(1)} %exchange.1.prod), custom_call_target="tpu_custom_call" | custom-call | tf_op jit(solution)/shard_map/turn/pallas_call | solution.py:409
